TPU v7x, 32 devices: a whole 2x2x4 slice. The times are simulated.
32 devices in a mesh: groups: 2 (over y), tile: 4 (over z), dp: 2 (over x), chan: 2 (over core).
Axes of the slice: x: 2, y: 2, z: 4, core: 2. Of those that a mesh axis runs over, the one named last changes fastest.
Arguments:
- activations: bfloat16 [8, 64, 32, 256], P(('groups', 'dp'), 'chan', 'tile'), parts along dimension 0, may hold values from -6 to 6
- occupancy: int32 [8, 4, 2, 2], P(('groups', 'dp'), 'tile'), parts along dimension 0, may hold values 0 or 1
- weight: bfloat16 [27, 64, 64], replicated, may hold values from -0.15625 to 0.15625
- cotangent: bfloat16 [8, 64, 32, 256], P(('groups', 'dp'), 'chan', 'tile'), parts along dimension 0, may hold values from -6 to 6
Outputs:
- output: bfloat16 [8, 64, 32, 256], P(('groups', 'dp'), 'chan', 'tile'), parts along dimension 0
- input_grad: bfloat16 [8, 64, 32, 256], P(('groups', 'dp'), 'chan', 'tile'), parts along dimension 0
- weight_grad: float32 [54, 64, 64], P('groups', 'chan'), parts along dimension 0
There are 2 independent parts, one for each index of `groups`. A program takes and returns all parts, laid end to end along the dimension named above; an argument that names none is the same for every part. Nothing has to cross between parts.
Inputs may be any that keep to these rules, and one draw needn't show every extreme that they name: `occupancy`: 1 marks a tile that holds tissue, 0 an empty one.
All inputs are finite; a program needn't handle non-finite values. No bound on the sum of `occupancy` on one device may be relied on, other than what follows from the above.
Results may differ from a plain program's by a relative error of at most 0.003.
Values may be sent and summed in bfloat16 or wider, within the bound.
A program may use at most 64 MiB of HBM per device.

v0:
```python
import math
import jax
import jax.numpy as jnp
from jax import lax
from jax.sharding import PartitionSpec as P

E = 8
GX = 2
GY = 2


def with_halo(cells, sides, width):
    for axis, dim in sides:
        count = lax.axis_size(axis)
        ends = count - 1
        head = lax.slice_in_dim(cells, 0, width, axis=dim)
        tail = lax.slice_in_dim(cells, cells.shape[dim] - width, cells.shape[dim], axis=dim)
        cells = jnp.concatenate(
            [
                lax.ppermute(tail, axis, [(i, (i + 1) % count) for i in range(ends)]),
                cells,
                lax.ppermute(head, axis, [((i + 1) % count, i) for i in range(ends)]),
            ],
            axis=dim,
        )
    return cells


def voxel_live(occupancy):
    batches, layers, tiles_x, tiles_y = occupancy.shape
    spread = jnp.broadcast_to(
        occupancy[:, :, None, :, None, :, None], (batches, layers, E, tiles_x, E, tiles_y, E)
    )
    return spread.reshape(batches, 1, layers * E, tiles_x * E * tiles_y * E)


def flat_padded(full):
    batches, channels, depth_rim, plane_size = full.shape
    width_y = GY * E
    flat = full.reshape(batches, channels, depth_rim * plane_size)
    return jnp.pad(flat, ((0, 0), (0, 0), (width_y + 1, width_y + 1)))


def shifted(padded, along_z, step_x, step_y, inner_len, plane_size):
    width_y = GY * E
    start = along_z * plane_size + (width_y + 1) + step_x * width_y + step_y
    return lax.slice_in_dim(padded, start, start + inner_len, axis=2)


def edge_mask(step_x, step_y, depth, plane_size):
    width_y = GY * E
    width_x = GX * E
    place = jnp.arange(plane_size, dtype=jnp.int32)
    row_x = place // width_y + step_x
    row_y = place % width_y + step_y
    valid = (row_x >= 0) & (row_x < width_x) & (row_y >= 0) & (row_y < width_y)
    return jnp.tile(valid.astype(jnp.float32), depth)


def shards(activations, occupancy, weight, cotangent):
    batches, own_channels, depth, plane_size = activations.shape
    inner_len = depth * plane_size
    own_start = lax.axis_index("chan") * own_channels
    weight_out = lax.dynamic_slice_in_dim(weight, own_start, own_channels, 1)
    weight_in = lax.dynamic_slice_in_dim(weight, own_start, own_channels, 2)
    live_mask = voxel_live(occupancy).astype(jnp.bfloat16)
    live_wide = live_mask.astype(jnp.float32)
    masked = activations * live_mask
    masked_rim = with_halo(masked, (("tile", 2),), 1)
    masked_full = lax.all_gather(masked_rim, "chan", axis=1, tiled=True)
    masked_flat = flat_padded(masked_full)
    summed = jnp.zeros((batches, own_channels, inner_len), jnp.float32)
    for plane_pos in range(9):
        along_x, along_y = (plane_pos // 3, plane_pos % 3)
        group_sum = jnp.zeros((batches, own_channels, inner_len), jnp.float32)
        for along_z in range(3):
            position = 9 * along_z + plane_pos
            source = shifted(masked_flat, along_z, along_x - 1, along_y - 1, inner_len, plane_size)
            group_sum = group_sum + jnp.einsum(
                "oi,siv->sov", weight_out[position], source, preferred_element_type=jnp.float32
            )
        summed = summed + edge_mask(along_x - 1, along_y - 1, depth, plane_size) * group_sum
    summed = summed.reshape(activations.shape)
    logistic = jax.nn.sigmoid(summed)
    output = (live_wide * (masked.astype(jnp.float32) + summed * logistic)).astype(jnp.bfloat16)
    slope = logistic * (1.0 + summed * (1.0 - logistic))
    grad_pre = (cotangent.astype(jnp.float32) * live_wide * slope).astype(jnp.bfloat16)
    grad_flat = grad_pre.reshape(batches, own_channels, inner_len)
    count = batches * lax.axis_size("dp") * depth * lax.axis_size("tile") * plane_size
    scale_factor = 1.0 / math.sqrt(count)
    grad_rim = with_halo(grad_pre, (("tile", 2),), 1)
    grad_full = lax.all_gather(grad_rim, "chan", axis=1, tiled=True)
    grad_padded = flat_padded(grad_full)
    back = jnp.zeros((batches, own_channels, inner_len), jnp.float32)
    for input_plane_pos in range(9):
        input_along_x, input_along_y = (input_plane_pos // 3, input_plane_pos % 3)
        group_sum = jnp.zeros((batches, own_channels, inner_len), jnp.float32)
        for input_along_z in range(3):
            input_position = 9 * input_along_z + input_plane_pos
            input_source = shifted(
                grad_padded,
                2 - input_along_z,
                1 - input_along_x,
                1 - input_along_y,
                inner_len,
                plane_size,
            )
            group_sum = group_sum + jnp.einsum(
                "oi,sov->siv",
                weight_in[input_position],
                input_source,
                preferred_element_type=jnp.float32,
            )
        back = back + edge_mask(1 - input_along_x, 1 - input_along_y, depth, plane_size) * group_sum
    back = back.reshape(activations.shape)
    input_grad = (live_wide * (cotangent.astype(jnp.float32) + back)).astype(jnp.bfloat16)
    pieces = [None] * 27
    for plane_pos in range(9):
        along_x, along_y = (plane_pos // 3, plane_pos % 3)
        border = edge_mask(along_x - 1, along_y - 1, depth, plane_size).astype(jnp.bfloat16)
        grad_edge = grad_flat * border
        for along_z in range(3):
            position = 9 * along_z + plane_pos
            source = shifted(masked_flat, along_z, along_x - 1, along_y - 1, inner_len, plane_size)
            pieces[position] = jnp.einsum(
                "sov,siv->oi", grad_edge, source, preferred_element_type=jnp.float32
            )
    local_term = jnp.stack(pieces)
    weight_grad = lax.psum(local_term, ("tile", "dp")) * scale_factor
    return (output, input_grad, weight_grad)


def solution(mesh):
    return jax.shard_map(
        shards,
        mesh=mesh,
        in_specs=(
            P(("groups", "dp"), "chan", "tile", None),
            P(("groups", "dp"), "tile", None, None),
            P(),
            P(("groups", "dp"), "chan", "tile", None),
        ),
        out_specs=(
            P(("groups", "dp"), "chan", "tile", None),
            P(("groups", "dp"), "chan", "tile", None),
            P("groups", "chan", None),
        ),
        check_vma=False,
    )
```

profile of v0, /device:TPU:0, one launch (start us, length us, event | category | flops | bytes accessed | tf_op | source)
XLA Modules:
  0.0 131.8 jit_solution(1393877452400870475)
XLA Ops:
  7.2 0.7 convert_bitcast_fusion
  8.1 1.0 broadcast_multiply_fusion.1
  9.2 4.9 %collective-permute-start = (bf16[2,32,1,256]{3,2,1,0:T(2,128)(2,1)S(1)}, bf16[2,32,1,256]{3,2,1,0:T(2,128)(2,1)S(1)}, u32[]{:S(2)}, u32[]{:S(2)}) collective-permute-start(bf16[2,32,1,256]{3,2,1,0:T(2,128)(2,1)S(1)} %get-tuple-element.7), channel_id=1, source_target_pairs={{0,4},{4,8},{8,12},{1,5},{5,9},{9,13},{2,6},{6,10},{10,14},{3,7},{... | collective-permute-start | bytes 98312 | tf_op jit(solution)/shard_map/ppermute | solution.py:20
  14.2 1.3 collective-permute-start.1
  16.0 4.3 %collective-permute-done.1 = bf16[2,32,1,256]{3,2,1,0:T(2,128)(2,1)S(1)} collective-permute-done((bf16[2,32,1,256]{3,2,1,0:T(2,128)(2,1)S(1)}, bf16[2,32,1,256]{3,2,1,0:T(2,128)(2,1)S(1)}, u32[]{:S(2)}, u32[]{:S(2)}) %collective-permute-start.1) | collective-permute-done | bytes 32800 | tf_op jit(solution)/shard_map/ppermute | solution.py:22
  20.6 2.6 %all_gather.6 = bf16[2,64,10,256]{3,2,1,0:T(8,128)(2,1)S(1)} all-gather(bf16[2,32,10,256]{3,2,1,0:T(8,128)(2,1)S(1)} %pad_maximum_fusion), channel_id=1, replica_groups=mesh['groups'=2,'tile'=4,'dp'=2,'chan'=2] {'chan'}, dimensions={1}, use_global_device_ids=true | all-gather | bytes 983040 | tf_op jit(solution)/shard_map/all_gather | solution.py:70
  23.2 0.4 reshape.170
  32.6 0.8 copy-done.1
  33.4 1.0 fusion.62
  39.5 0.4 fusion.46
  43.8 3.5 %collective-permute-start.2 = (bf16[2,32,1,256]{3,2,1,0:T(2,128)(2,1)S(1)}, bf16[2,32,1,256]{3,2,1,0:T(2,128)(2,1)S(1)}, u32[]{:S(2)}, u32[]{:S(2)}) collective-permute-start(bf16[2,32,1,256]{3,2,1,0:T(2,128)(2,1)S(1)} %get-tuple-element.5), channel_id=1, source_target_pairs={{0,4},{4,8},{8,12},{1,5},{5,9},{9,13},{2,6},{6,10},{10,14},{3,7},{... | collective-permute-start | bytes 98312 | tf_op jit(solution)/shard_map/ppermute | solution.py:20
  47.3 1.3 collective-permute-start.3
  49.0 0.8 copy-done.3
  49.8 3.7 %collective-permute-done.3 = bf16[2,32,1,256]{3,2,1,0:T(2,128)(2,1)S(1)} collective-permute-done((bf16[2,32,1,256]{3,2,1,0:T(2,128)(2,1)S(1)}, bf16[2,32,1,256]{3,2,1,0:T(2,128)(2,1)S(1)}, u32[]{:S(2)}, u32[]{:S(2)}) %collective-permute-start.3) | collective-permute-done | bytes 32800 | tf_op jit(solution)/shard_map/ppermute | solution.py:22
  53.8 2.6 %all_gather.7 = bf16[2,64,10,256]{3,2,1,0:T(8,128)(2,1)S(1)} all-gather(bf16[2,32,10,256]{3,2,1,0:T(8,128)(2,1)S(1)} %pad_maximum_fusion.1), channel_id=1, replica_groups=mesh['groups'=2,'tile'=4,'dp'=2,'chan'=2] {'chan'}, dimensions={1}, use_global_device_ids=true | all-gather | bytes 983040 | tf_op jit(solution)/shard_map/all_gather | solution.py:92
  56.4 0.4 reshape.172
  59.0 0.4 fusion.83
  61.3 0.4 fusion.7
  62.8 0.4 fusion.5
  66.1 0.4 fusion.30
  66.6 0.4 fusion.33
  67.1 0.8 fusion.64
  67.9 55.2 %all-reduce.4.cloned.1.call-done = f32[27,32,64]{2,1,0:T(8,128)} async-done(((f32[27,32,64]{2,1,0:T(8,128)}), f32[27,32,64]{2,1,0:T(8,128)}) %all-reduce.4.cloned.1.call-update) | async-done | bytes 221200 | tf_op jit(solution)/shard_map/psum | solution.py:129
  123.1 1.8 %broadcast_multiply_fusion = f32[27,32,64]{2,1,0:T(8,128)} fusion(f32[27,32,64]{2,1,0:T(8,128)} %all-reduce.4.cloned.1.call-done), kind=kLoop, calls=%fused_computation.250 | loop fusion | flops 55296 | bytes 442368 | tf_op jit(solution)/shard_map/mul | solution.py:129
  (127 shorter events, 27.8 us)
Async XLA Ops:
  7.2 16.4 %copy-start = (bf16[27,64,64]{2,1,0:T(8,128)(2,1)S(1)}, bf16[27,64,64]{2,1,0:T(8,128)(2,1)}, u32[]{:S(2)}) copy-start(bf16[27,64,64]{2,1,0:T(8,128)(2,1)} %param.6) | copy-start | bytes 663556
  7.2 116.0 %all-reduce.4.cloned.1.call-start = ((), (), s32[]{:S(2)}) async-start(), calls=%async_computation | async-start | bytes 884736 | tf_op jit(solution)/shard_map/psum | solution.py:129
  9.2 6.8 %collective-permute-start = (bf16[2,32,1,256]{3,2,1,0:T(2,128)(2,1)S(1)}, bf16[2,32,1,256]{3,2,1,0:T(2,128)(2,1)S(1)}, u32[]{:S(2)}, u32[]{:S(2)}) collective-permute-start(bf16[2,32,1,256]{3,2,1,0:T(2,128)(2,1)S(1)} %get-tuple-element.7), channel_id=1, source_target_pairs={{0,4},{4,8},{8,12},{1,5},{5,9},{9,13},{2,6},{6,10},{10,14},{3,7},{... | collective-permute-start | bytes 98312 | tf_op jit(solution)/shard_map/ppermute | solution.py:20
  14.2 6.2 %collective-permute-start.1 = (bf16[2,32,1,256]{3,2,1,0:T(2,128)(2,1)S(1)}, bf16[2,32,1,256]{3,2,1,0:T(2,128)(2,1)S(1)}, u32[]{:S(2)}, u32[]{:S(2)}) collective-permute-start(bf16[2,32,1,256]{3,2,1,0:T(2,128)(2,1)S(1)} %get-tuple-element.8), channel_id=1, source_target_pairs={{4,0},{8,4},{12,8},{5,1},{9,5},{13,9},{6,2},{10,6},{14,10},{7,3},{... | collective-permute-start | bytes 98312 | tf_op jit(solution)/shard_map/ppermute | solution.py:22
  32.4 1.0 copy-start.1
  32.4 1.0 copy-start.2
  43.8 5.9 %collective-permute-start.2 = (bf16[2,32,1,256]{3,2,1,0:T(2,128)(2,1)S(1)}, bf16[2,32,1,256]{3,2,1,0:T(2,128)(2,1)S(1)}, u32[]{:S(2)}, u32[]{:S(2)}) collective-permute-start(bf16[2,32,1,256]{3,2,1,0:T(2,128)(2,1)S(1)} %get-tuple-element.5), channel_id=1, source_target_pairs={{0,4},{4,8},{8,12},{1,5},{5,9},{9,13},{2,6},{6,10},{10,14},{3,7},{... | collective-permute-start | bytes 98312 | tf_op jit(solution)/shard_map/ppermute | solution.py:20
  47.3 6.2 %collective-permute-start.3 = (bf16[2,32,1,256]{3,2,1,0:T(2,128)(2,1)S(1)}, bf16[2,32,1,256]{3,2,1,0:T(2,128)(2,1)S(1)}, u32[]{:S(2)}, u32[]{:S(2)}) collective-permute-start(bf16[2,32,1,256]{3,2,1,0:T(2,128)(2,1)S(1)} %get-tuple-element.6), channel_id=1, source_target_pairs={{4,0},{8,4},{12,8},{5,1},{9,5},{13,9},{6,2},{10,6},{14,10},{7,3},{... | collective-permute-start | bytes 98312 | tf_op jit(solution)/shard_map/ppermute | solution.py:22
  49.0 0.8 copy-start.3
Sparse Core Ops, SparseCore 0:
  49.9 73.1 all-reduce.3
where the time goes:
time: 132 us
  waiting for transfers between devices  63.4 us (48%)
  matrix products  28.2 us (21%)
  between operations  14.7 us (11%)
  starting transfers between devices  11 us (8%)
  other arithmetic  6.03 us (5%)
  blocking collectives  5.11 us (4%)
  local copies, waits for them, and re-layouts  3.32 us (3%)
    psum x1, waiting for transfers between devices, shards(): weight_grad = lax.psum(local_term, ('tile', 'dp')) * scale_factor  55.2 us
    dot_general x27, matrix products, shards(): jnp.einsum('oi,sov->siv', weight_in[input_position], input_source, prefer...  9.99 us
    dot_general x27, matrix products, shards(): jnp.einsum('sov,siv->oi', grad_edge, source, preferred_element_type=jnp.f...  9.54 us
    dot_general x27, matrix products, shards(): jnp.einsum('oi,siv->sov', weight_out[position], source, preferred_element...  8.68 us
    ppermute x2, starting transfers between devices, with_halo(): lax.ppermute(tail, axis, [(i, (i + 1) % count) for i in range(ends)])  8.42 us
    ppermute x2, waiting for transfers between devices, with_halo(): lax.ppermute(head, axis, [((i + 1) % count, i) for i in range(ends)])  7.98 us
  transfers between devices with their start and end apart: 5, of which 4 were waited for; matrix products, arithmetic and copies ran while one was open for 9% of the time, Pallas kernels for 0%

commit v1 on v0

--- a/solution.py
+++ b/solution.py
@@ -126,7 +126,7 @@
                 "sov,siv->oi", grad_edge, source, preferred_element_type=jnp.float32
             )
     local_term = jnp.stack(pieces)
-    weight_grad = lax.psum(local_term, ("tile", "dp")) * scale_factor
+    weight_grad = jnp.sum(lax.all_gather(local_term, ("tile", "dp")), axis=0) * scale_factor
     return (output, input_grad, weight_grad)
 
 

time: 132 us -> 126 us (0.955)
  waiting for transfers between devices: 63.4 us -> 56.7 us
  other arithmetic: 6.03 us -> 7.51 us
    psum x1 -> x0, waiting for transfers between devices: 55.2 us -> none  [shards(): weight_grad = lax.psum(local_term, ('tile', 'dp')) * scale_factor]
    all_gather x0 -> x1, waiting for transfers between devices: none -> 48.5 us  [shards(): lax.all_gather(local_term, ('tile', 'dp'))]
    reduce_sum x0 -> x1, other arithmetic: none -> 2.48 us  [shards(): jnp.sum(lax.all_gather(local_term, ('tile', 'dp')), axis=0) * scale_factor]
  transfers between devices with their start and end apart: 5 -> 5, of which waited for: 4 -> 4; matrix products, arithmetic and copies ran while one was open for 9% -> 10% of each run, Pallas kernels for 0% -> 0%
where the time goes in v1:
time: 126 us
  waiting for transfers between devices  56.7 us (45%)
  matrix products  28.2 us (22%)
  between operations  14.7 us (12%)
  starting transfers between devices  11 us (9%)
  other arithmetic  7.51 us (6%)
  blocking collectives  5.11 us (4%)
  local copies, waits for them, and re-layouts  2.49 us (2%)
    all_gather x1, waiting for transfers between devices, shards(): lax.all_gather(local_term, ('tile', 'dp'))  48.5 us
    dot_general x27, matrix products, shards(): jnp.einsum('oi,sov->siv', weight_in[input_position], input_source, prefer...  9.97 us
    dot_general x27, matrix products, shards(): jnp.einsum('sov,siv->oi', grad_edge, source, preferred_element_type=jnp.f...  9.54 us
    dot_general x27, matrix products, shards(): jnp.einsum('oi,siv->sov', weight_out[position], source, preferred_element...  8.68 us
    ppermute x2, starting transfers between devices, with_halo(): lax.ppermute(tail, axis, [(i, (i + 1) % count) for i in range(ends)])  8.42 us
    ppermute x2, waiting for transfers between devices, with_halo(): lax.ppermute(head, axis, [((i + 1) % count, i) for i in range(ends)])  7.98 us
    ppermute x2, starting transfers between devices, with_halo(): lax.ppermute(head, axis, [((i + 1) % count, i) for i in range(ends)])  2.58 us
    all_gather x1, blocking collectives, shards(): masked_full = lax.all_gather(masked_rim, 'chan', axis=1, tiled=True)  2.56 us
  transfers between devices with their start and end apart: 5, of which 4 were waited for; matrix products, arithmetic and copies ran while one was open for 10% of the time, Pallas kernels for 0%

profile of v1, /device:TPU:0, one launch (start us, length us, event | category | flops | bytes accessed | tf_op | source)
XLA Modules:
  0.0 125.7 jit_solution(13604915694421537116)
XLA Ops:
  7.2 0.7 convert_bitcast_fusion
  8.1 1.0 broadcast_multiply_fusion.1
  9.2 4.9 %collective-permute-start = (bf16[2,32,1,256]{3,2,1,0:T(2,128)(2,1)S(1)}, bf16[2,32,1,256]{3,2,1,0:T(2,128)(2,1)S(1)}, u32[]{:S(2)}, u32[]{:S(2)}) collective-permute-start(bf16[2,32,1,256]{3,2,1,0:T(2,128)(2,1)S(1)} %get-tuple-element.7), channel_id=1, source_target_pairs={{0,4},{4,8},{8,12},{1,5},{5,9},{9,13},{2,6},{6,10},{10,14},{3,7},{... | collective-permute-start | bytes 98312 | tf_op jit(solution)/shard_map/ppermute | solution.py:20
  14.2 1.3 %collective-permute-start.1 = (bf16[2,32,1,256]{3,2,1,0:T(2,128)(2,1)S(1)}, bf16[2,32,1,256]{3,2,1,0:T(2,128)(2,1)S(1)}, u32[]{:S(2)}, u32[]{:S(2)}) collective-permute-start(bf16[2,32,1,256]{3,2,1,0:T(2,128)(2,1)S(1)} %get-tuple-element.8), channel_id=1, source_target_pairs={{4,0},{8,4},{12,8},{5,1},{9,5},{13,9},{6,2},{10,6},{14,10},{7,3},{... | collective-permute-start | bytes 98312 | tf_op jit(solution)/shard_map/ppermute | solution.py:22
  16.0 4.3 %collective-permute-done.1 = bf16[2,32,1,256]{3,2,1,0:T(2,128)(2,1)S(1)} collective-permute-done((bf16[2,32,1,256]{3,2,1,0:T(2,128)(2,1)S(1)}, bf16[2,32,1,256]{3,2,1,0:T(2,128)(2,1)S(1)}, u32[]{:S(2)}, u32[]{:S(2)}) %collective-permute-start.1) | collective-permute-done | bytes 32800 | tf_op jit(solution)/shard_map/ppermute | solution.py:22
  20.6 2.6 %all_gather.12 = bf16[2,64,10,256]{3,2,1,0:T(8,128)(2,1)S(1)} all-gather(bf16[2,32,10,256]{3,2,1,0:T(8,128)(2,1)S(1)} %pad_maximum_fusion), channel_id=1, replica_groups=mesh['groups'=2,'tile'=4,'dp'=2,'chan'=2] {'chan'}, dimensions={1}, use_global_device_ids=true | all-gather | bytes 983040 | tf_op jit(solution)/shard_map/all_gather | solution.py:70
  23.2 0.4 reshape.170
  32.6 1.0 fusion.62
  38.7 0.4 fusion.46
  43.0 3.5 %collective-permute-start.2 = (bf16[2,32,1,256]{3,2,1,0:T(2,128)(2,1)S(1)}, bf16[2,32,1,256]{3,2,1,0:T(2,128)(2,1)S(1)}, u32[]{:S(2)}, u32[]{:S(2)}) collective-permute-start(bf16[2,32,1,256]{3,2,1,0:T(2,128)(2,1)S(1)} %get-tuple-element.5), channel_id=1, source_target_pairs={{0,4},{4,8},{8,12},{1,5},{5,9},{9,13},{2,6},{6,10},{10,14},{3,7},{... | collective-permute-start | bytes 98312 | tf_op jit(solution)/shard_map/ppermute | solution.py:20
  46.5 1.3 %collective-permute-start.3 = (bf16[2,32,1,256]{3,2,1,0:T(2,128)(2,1)S(1)}, bf16[2,32,1,256]{3,2,1,0:T(2,128)(2,1)S(1)}, u32[]{:S(2)}, u32[]{:S(2)}) collective-permute-start(bf16[2,32,1,256]{3,2,1,0:T(2,128)(2,1)S(1)} %get-tuple-element.6), channel_id=1, source_target_pairs={{4,0},{8,4},{12,8},{5,1},{9,5},{13,9},{6,2},{10,6},{14,10},{7,3},{... | collective-permute-start | bytes 98312 | tf_op jit(solution)/shard_map/ppermute | solution.py:22
  48.2 0.8 copy-done.3
  49.0 3.7 %collective-permute-done.3 = bf16[2,32,1,256]{3,2,1,0:T(2,128)(2,1)S(1)} collective-permute-done((bf16[2,32,1,256]{3,2,1,0:T(2,128)(2,1)S(1)}, bf16[2,32,1,256]{3,2,1,0:T(2,128)(2,1)S(1)}, u32[]{:S(2)}, u32[]{:S(2)}) %collective-permute-start.3) | collective-permute-done | bytes 32800 | tf_op jit(solution)/shard_map/ppermute | solution.py:22
  53.0 2.6 %all_gather.13 = bf16[2,64,10,256]{3,2,1,0:T(8,128)(2,1)S(1)} all-gather(bf16[2,32,10,256]{3,2,1,0:T(8,128)(2,1)S(1)} %pad_maximum_fusion.1), channel_id=1, replica_groups=mesh['groups'=2,'tile'=4,'dp'=2,'chan'=2] {'chan'}, dimensions={1}, use_global_device_ids=true | all-gather | bytes 983040 | tf_op jit(solution)/shard_map/all_gather | solution.py:92
  55.6 0.4 reshape.172
  56.0 0.4 fusion.80
  57.8 0.4 fusion.83
  64.2 0.4 fusion.6
  65.3 0.4 fusion.30
  65.7 0.4 fusion.33
  66.3 0.8 fusion.64
  67.1 48.5 %all-gather.3.cloned.1.call-done = f32[216,32,64]{2,1,0:T(8,128)} async-done(((f32[27,32,64]{2,1,0:T(8,128)}), f32[216,32,64]{2,1,0:T(8,128)}) %all-gather.3.cloned.1.call-update) | async-done | bytes 1769488 | tf_op jit(solution)/shard_map/all_gather | solution.py:129
  115.6 2.5 %reduce_sum.9 = f32[27,32,64]{2,1,0:T(8,128)S(1)} reduce(f32[8,27,32,64]{3,2,1,0:T(8,128)} %bitcast.448, f32[]{:T(128)} %constant.196.clone.1), dimensions={0}, to_apply=%region_0.1 | reduce | flops 387072 | bytes 1990660 | tf_op jit(solution)/shard_map/reduce_sum | solution.py:129
  118.1 0.8 broadcast_multiply_fusion
  (128 shorter events, 27.7 us)
Async XLA Ops:
  7.2 16.4 %copy-start = (bf16[27,64,64]{2,1,0:T(8,128)(2,1)S(1)}, bf16[27,64,64]{2,1,0:T(8,128)(2,1)}, u32[]{:S(2)}) copy-start(bf16[27,64,64]{2,1,0:T(8,128)(2,1)} %param.6) | copy-start | bytes 663556
  7.2 108.4 %all-gather.3.cloned.1.call-start = ((), (), s32[]{:S(2)}) async-start(), calls=%async_computation | async-start | bytes 3981312 | tf_op jit(solution)/shard_map/all_gather | solution.py:129
  9.2 6.8 %collective-permute-start = (bf16[2,32,1,256]{3,2,1,0:T(2,128)(2,1)S(1)}, bf16[2,32,1,256]{3,2,1,0:T(2,128)(2,1)S(1)}, u32[]{:S(2)}, u32[]{:S(2)}) collective-permute-start(bf16[2,32,1,256]{3,2,1,0:T(2,128)(2,1)S(1)} %get-tuple-element.7), channel_id=1, source_target_pairs={{0,4},{4,8},{8,12},{1,5},{5,9},{9,13},{2,6},{6,10},{10,14},{3,7},{... | collective-permute-start | bytes 98312 | tf_op jit(solution)/shard_map/ppermute | solution.py:20
  14.2 6.2 %collective-permute-start.1 = (bf16[2,32,1,256]{3,2,1,0:T(2,128)(2,1)S(1)}, bf16[2,32,1,256]{3,2,1,0:T(2,128)(2,1)S(1)}, u32[]{:S(2)}, u32[]{:S(2)}) collective-permute-start(bf16[2,32,1,256]{3,2,1,0:T(2,128)(2,1)S(1)} %get-tuple-element.8), channel_id=1, source_target_pairs={{4,0},{8,4},{12,8},{5,1},{9,5},{13,9},{6,2},{10,6},{14,10},{7,3},{... | collective-permute-start | bytes 98312 | tf_op jit(solution)/shard_map/ppermute | solution.py:22
  31.3 1.2 copy-start.1
  31.3 1.2 copy-start.2
  43.0 5.9 %collective-permute-start.2 = (bf16[2,32,1,256]{3,2,1,0:T(2,128)(2,1)S(1)}, bf16[2,32,1,256]{3,2,1,0:T(2,128)(2,1)S(1)}, u32[]{:S(2)}, u32[]{:S(2)}) collective-permute-start(bf16[2,32,1,256]{3,2,1,0:T(2,128)(2,1)S(1)} %get-tuple-element.5), channel_id=1, source_target_pairs={{0,4},{4,8},{8,12},{1,5},{5,9},{9,13},{2,6},{6,10},{10,14},{3,7},{... | collective-permute-start | bytes 98312 | tf_op jit(solution)/shard_map/ppermute | solution.py:20
  46.5 6.2 %collective-permute-start.3 = (bf16[2,32,1,256]{3,2,1,0:T(2,128)(2,1)S(1)}, bf16[2,32,1,256]{3,2,1,0:T(2,128)(2,1)S(1)}, u32[]{:S(2)}, u32[]{:S(2)}) collective-permute-start(bf16[2,32,1,256]{3,2,1,0:T(2,128)(2,1)S(1)} %get-tuple-element.6), channel_id=1, source_target_pairs={{4,0},{8,4},{12,8},{5,1},{9,5},{13,9},{6,2},{10,6},{14,10},{7,3},{... | collective-permute-start | bytes 98312 | tf_op jit(solution)/shard_map/ppermute | solution.py:22
  48.2 0.8 copy-start.3
Sparse Core Ops, SparseCore 0:
  49.1 66.4 all-gather.2
